TPU v7x, 256 devices: a whole 4x4x8 slice. The times are simulated.
256 devices in a mesh: rep: 64 (over z, x_hi, y), fsdp: 4 (over x_lo, core).
Axes of the slice: x: 4 (x_hi: 2, x_lo: 2; x = x_hi * 2 + x_lo), y: 4, z: 8, core: 2. Of those that a mesh axis runs over, the one named last changes fastest.
Arguments:
- inputs: bfloat16 [64, 2, 512, 2048], P('rep', None, 'fsdp'), may hold values from -6 to 6
- cotangent: bfloat16 [64, 2, 512, 2048], P('rep', None, 'fsdp'), may hold values from -6 to 6
- mid_gain: float32 [2048], replicated, may hold values from 0.5 to 1.5
- out_gain: float32 [2048], replicated, may hold values from 0.5 to 1.5
- up_weight: bfloat16 [64, 2048, 3584], P('rep', None, 'fsdp'), may hold values from -6 to 6
- down_weight: bfloat16 [64, 2048, 3584], P('rep', None, 'fsdp'), may hold values from -6 to 6
- up_rows: float32 [64, 2048], P('rep'), may hold values from 1e-09 to 1e-06
- up_cols: float32 [64, 3584], P('rep', 'fsdp'), may hold values from 1e-09 to 1e-06
- down_rows: float32 [64, 2048], P('rep'), may hold values from 1e-09 to 1e-06
- down_cols: float32 [64, 3584], P('rep', 'fsdp'), may hold values from 1e-09 to 1e-06
- anchor_up: float32 [2048, 512], P('rep', 'fsdp'), may hold values from -6 to 6
- anchor_down: float32 [2048, 512], P('rep', 'fsdp'), may hold values from -6 to 6
- momentum_up: float32 [2048, 512], P('rep', 'fsdp'), may hold values from -4 to 4
- momentum_down: float32 [2048, 512], P('rep', 'fsdp'), may hold values from -4 to 4
- fragment: int32 [1], replicated, may hold values from 0 to 6
Outputs:
- merged_up: bfloat16 [64, 2048, 512], P('rep', None, 'fsdp')
- merged_down: bfloat16 [64, 2048, 512], P('rep', None, 'fsdp')
- central_up: float32 [2048, 512], P('rep', 'fsdp')
- central_down: float32 [2048, 512], P('rep', 'fsdp')
- velocity_up: float32 [2048, 512], P('rep', 'fsdp')
- velocity_down: float32 [2048, 512], P('rep', 'fsdp')
- token_loss: float32 [64, 2, 512], P('rep', None, 'fsdp')
All inputs are finite; a program needn't handle non-finite values.
Results may differ from a plain program's by a relative error of at most 0.002.
The roundings to bfloat16 on the way count: a program that leaves them out, or rounds other values in their place, can miss the bound.
Values may be sent and summed in bfloat16 or wider, within the bound.
A program may use at most 128 MiB of HBM per device.

v0:
```python
import math

import jax
import jax.numpy as jnp
from jax import lax
from jax.sharding import PartitionSpec as P

norm_epsilon = 1e-05
row_decay = 0.95
inner_rate = 0.05
weight_decay = 0.1
outer_rate = 0.7
outer_momentum = 0.9
mixing = 0.5


def normalize(values, gain):
    factor = lax.rsqrt(jnp.mean(values * values, axis=-1, keepdims=True) + norm_epsilon)
    return (values * factor * gain, factor)


def outer_update(anchor, momentum, drift):
    velocity = outer_momentum * momentum + drift
    central = anchor - outer_rate * (drift + outer_momentum * velocity)
    return (central, velocity)


def contract_tokens(left, right):
    return lax.dot_general(
        left, right, (((0,), (0,)), ((), ())), preferred_element_type=jnp.float32
    )


def layer(inputs_now, cot_now, mid_gain, out_gain, up_now, down_now, shards):
    width, local_units = up_now.shape
    units = local_units * shards
    residual = inputs_now.astype(jnp.float32)
    normed, mid_factor = normalize(residual, mid_gain)
    normed_low = normed.astype(jnp.bfloat16)
    normed_all = lax.all_gather(normed_low, "fsdp", axis=0, tiled=True)
    preact = jnp.dot(normed_all, up_now, preferred_element_type=jnp.float32) * (
        1.0 / math.sqrt(width)
    )
    logistic = jax.nn.sigmoid(preact)
    hidden = (preact * logistic).astype(jnp.bfloat16)
    branch = lax.psum_scatter(
        lax.dot_general(
            hidden, down_now, (((1,), (1,)), ((), ())), preferred_element_type=jnp.float32
        ),
        "fsdp",
        scatter_dimension=0,
        tiled=True,
    )
    output = residual + branch * (1.0 / math.sqrt(units))
    final, out_factor = normalize(output, out_gain)
    losses = jnp.sum(cot_now.astype(jnp.float32) * final, axis=-1)
    return (losses, (normed_all, preact, logistic, hidden, output, out_factor, cot_now))


def factored_update(weight, rows, cols, gradient, row_total, units):
    squared = gradient * gradient
    rows_new = row_decay * rows + (1 - row_decay) * row_total / units
    cols_new = row_decay * cols + (1 - row_decay) * jnp.mean(squared, axis=0)
    estimate = rows_new[:, None] * cols_new[None, :] / jnp.mean(rows_new)
    weight_full = weight.astype(jnp.float32)
    weight_full = weight_full - inner_rate * (
        gradient * lax.rsqrt(estimate) + weight_decay * weight_full
    )
    return weight_full.astype(jnp.bfloat16)


def per_device(
    inputs,
    cotangent,
    mid_gain,
    out_gain,
    up_weight,
    down_weight,
    up_rows,
    up_cols,
    down_rows,
    down_cols,
    anchor_up,
    anchor_down,
    momentum_up,
    momentum_down,
    fragment,
):
    shards = lax.axis_size("fsdp")
    replicas = lax.axis_size("rep")
    up_now, down_now = (up_weight[0], down_weight[0])
    width, local_units = up_now.shape
    units = local_units * shards
    tok_rows = inputs.shape[2]
    token_count = tok_rows * shards
    block_width = anchor_up.shape[1]
    share_rows = anchor_up.shape[0]
    offset = fragment[0] * block_width
    start_up = lax.dynamic_slice_in_dim(up_now, offset, block_width, 1).astype(jnp.float32)
    start_down = lax.dynamic_slice_in_dim(down_now, offset, block_width, 1).astype(jnp.float32)
    total_up, total_down = lax.psum((start_up, start_down), "rep")
    whole_anchor_up, whole_anchor_down, whole_moment_up, whole_moment_down = (
        lax.all_gather(anchor_up, "rep", axis=0, tiled=True),
        lax.all_gather(anchor_down, "rep", axis=0, tiled=True),
        lax.all_gather(momentum_up, "rep", axis=0, tiled=True),
        lax.all_gather(momentum_down, "rep", axis=0, tiled=True),
    )
    full_central_up, full_velocity_up = outer_update(
        whole_anchor_up, whole_moment_up, whole_anchor_up - total_up / replicas
    )
    full_central_down, full_velocity_down = outer_update(
        whole_anchor_down, whole_moment_down, whole_anchor_down - total_down / replicas
    )
    row_start = lax.axis_index("rep") * share_rows
    central_up = lax.dynamic_slice_in_dim(full_central_up, row_start, share_rows, 0)
    central_down = lax.dynamic_slice_in_dim(full_central_down, row_start, share_rows, 0)
    velocity_up = lax.dynamic_slice_in_dim(full_velocity_up, row_start, share_rows, 0)
    velocity_down = lax.dynamic_slice_in_dim(full_velocity_down, row_start, share_rows, 0)
    first, saved = layer(
        inputs[0, 0], cotangent[0, 0], mid_gain, out_gain, up_now, down_now, shards
    )
    normed_all, preact, logistic, hidden, output, out_factor, cot_rows = saved
    gscaled = cot_rows.astype(jnp.float32) * (1.0 / token_count) * out_gain
    doutput = out_factor * gscaled - output * out_factor**3 * jnp.mean(
        output * gscaled, axis=-1, keepdims=True
    )
    dbranch = (doutput * (1.0 / math.sqrt(units))).astype(jnp.bfloat16)
    dbranch_all = lax.all_gather(dbranch, "fsdp", axis=0, tiled=True)
    grad_down = contract_tokens(dbranch_all, hidden)
    dhidden = jnp.dot(dbranch_all, down_now, preferred_element_type=jnp.float32)
    dpre = (dhidden * logistic * (1 + preact * (1 - logistic)) * (1.0 / math.sqrt(width))).astype(
        jnp.bfloat16
    )
    grad_up = contract_tokens(normed_all, dpre)
    total_rows_up, total_rows_down = lax.psum(
        (jnp.sum(grad_up * grad_up, axis=1), jnp.sum(grad_down * grad_down, axis=1)), "fsdp"
    )
    up_new = factored_update(up_now, up_rows[0], up_cols[0], grad_up, total_rows_up, units)
    down_new = factored_update(
        down_now, down_rows[0], down_cols[0], grad_down, total_rows_down, units
    )
    second = layer(inputs[0, 1], cotangent[0, 1], mid_gain, out_gain, up_new, down_new, shards)[0]
    block_up = lax.dynamic_slice_in_dim(up_new, offset, block_width, 1).astype(jnp.float32)
    block_down = lax.dynamic_slice_in_dim(down_new, offset, block_width, 1).astype(jnp.float32)
    merged_up = (mixing * block_up + (1 - mixing) * full_central_up).astype(jnp.bfloat16)
    merged_down = (mixing * block_down + (1 - mixing) * full_central_down).astype(jnp.bfloat16)
    token_loss = jnp.stack([first, second])[None]
    return (
        merged_up[None],
        merged_down[None],
        central_up,
        central_down,
        velocity_up,
        velocity_down,
        token_loss,
    )


def solution(mesh):
    placed = (
        P("rep", None, "fsdp", None),
        P("rep", None, "fsdp", None),
        P(),
        P(),
        P("rep", None, "fsdp"),
        P("rep", None, "fsdp"),
        P("rep", None),
        P("rep", "fsdp"),
        P("rep", None),
        P("rep", "fsdp"),
        P("rep", "fsdp"),
        P("rep", "fsdp"),
        P("rep", "fsdp"),
        P("rep", "fsdp"),
        P(),
    )
    return jax.shard_map(
        per_device,
        mesh=mesh,
        in_specs=placed,
        out_specs=(
            P("rep", None, "fsdp"),
            P("rep", None, "fsdp"),
            P("rep", "fsdp"),
            P("rep", "fsdp"),
            P("rep", "fsdp"),
            P("rep", "fsdp"),
            P("rep", None, "fsdp"),
        ),
        check_vma=False,
    )
```

profile of v0, /device:TPU:1, one launch (start us, length us, event | category | flops | bytes accessed | tf_op | source)
XLA Modules:
  0.0 1402.1 jit_solution(10205428838352137670)
XLA Ops:
  7.2 1.2 fusion.21
  8.4 2.0 fusion.23
  10.6 36.0 %all-gather.8.cloned.1.call-done = bf16[512,2048]{1,0:T(8,128)(2,1)} async-done(((bf16[128,2048]{1,0:T(8,128)(2,1)}), bf16[512,2048]{1,0:T(8,128)(2,1)}) %all-gather.8.cloned.1.call-update) | async-done | bytes 2097168 | tf_op jit(solution)/shard_map/all_gather | solution.py:40
  46.5 5.1 fusion.10
  51.7 1.2 copy-done.12
  53.0 4.3 fusion.8
  58.0 48.1 %reduce-scatter.3.cloned.1.call-done = f32[128,2048]{1,0:T(8,128)} async-done(((f32[512,2048]{1,0:T(8,128)}), f32[128,2048]{1,0:T(8,128)}) %reduce-scatter.3.cloned.1.call-update) | async-done | bytes 1048592 | tf_op jit(solution)/shard_map/reduce_scatter | solution.py:46
  106.1 1.6 multiply_reduce_fusion.5
  107.7 1.9 fusion.20
  109.6 1.5 fusion.26
  113.6 2.7 bitcast_convert_fusion
  116.3 0.7 all-gather.12.cloned.1.call-update
  117.1 0.7 all-gather.14.cloned.1.call-update
  118.0 26.0 %all-gather.10.cloned.1.call-done = bf16[512,2048]{1,0:T(8,128)(2,1)} async-done(((bf16[128,2048]{1,0:T(8,128)(2,1)}), bf16[512,2048]{1,0:T(8,128)(2,1)}) %all-gather.10.cloned.1.call-update) | async-done | bytes 2097168 | tf_op jit(solution)/shard_map/all_gather | solution.py:128
  144.1 7.7 multiply_reduce_fusion
  151.8 11.6 multiply_reduce_fusion.2
  163.4 10.5 all-reduce.1
  176.5 6.8 fusion.5
  183.3 0.9 slice-done.1
  184.1 1.0 copy-done.3
  185.2 3.6 fusion.2
  188.8 10.3 fusion.31
  199.2 94.4 %all-gather.16.cloned.1.call-done = f32[2048,128]{1,0:T(8,128)} async-done(((f32[32,128]{1,0:T(8,128)}), f32[2048,128]{1,0:T(8,128)}) %all-gather.16.cloned.1.call-update) | async-done | bytes 1048592 | tf_op jit(solution)/shard_map/all_gather | solution.py:104
  293.6 115.0 %all-gather.18.cloned.1.call-done = f32[2048,128]{1,0:T(8,128)} async-done(((f32[32,128]{1,0:T(8,128)}), f32[2048,128]{1,0:T(8,128)}) %all-gather.18.cloned.1.call-update) | async-done | bytes 1048592 | tf_op jit(solution)/shard_map/all_gather | solution.py:106
  408.6 659.5 %all-reduce.4.cloned.1.call-done = (f32[2048,128]{1,0:T(8,128)}, f32[2048,128]{1,0:T(8,128)}) async-done(((f32[2048,128]{1,0:T(8,128)}, f32[2048,128]{1,0:T(8,128)}), (f32[2048,128]{1,0:T(8,128)}, f32[2048,128]{1,0:T(8,128)})) %all-reduce.4.cloned.1.call-update) | async-done | bytes 2097168 | tf_op jit(solution)/shard_map/psum | solution.py:101
  1068.1 3.3 fusion.33
  1072.6 152.5 %all-gather.12.cloned.1.call-done = f32[2048,128]{1,0:T(8,128)} async-done(((f32[32,128]{1,0:T(8,128)}), f32[2048,128]{1,0:T(8,128)}) %all-gather.12.cloned.1.call-update) | async-done | bytes 1048592 | tf_op jit(solution)/shard_map/all_gather | solution.py:103
  1225.2 114.6 %all-gather.14.cloned.1.call-done = f32[2048,128]{1,0:T(8,128)} async-done(((f32[32,128]{1,0:T(8,128)}), f32[2048,128]{1,0:T(8,128)}) %all-gather.14.cloned.1.call-update) | async-done | bytes 1048592 | tf_op jit(solution)/shard_map/all_gather | solution.py:105
  1339.8 2.9 fusion.32
  1343.9 47.6 %reduce-scatter.5.cloned.1.call-done = f32[128,2048]{1,0:T(8,128)} async-done(((f32[512,2048]{1,0:T(8,128)}), f32[128,2048]{1,0:T(8,128)}) %reduce-scatter.5.cloned.1.call-update) | async-done | bytes 1048592 | tf_op jit(solution)/shard_map/reduce_scatter | solution.py:46
  1391.5 1.5 multiply_reduce_fusion.4
  1393.0 1.6 fusion.27
  (65 shorter events, 7.2 us)
Async XLA Ops:
  7.2 39.4 %all-gather.8.cloned.1.call-start = ((), (), s32[]{:S(2)}) async-start(), calls=%async_computation.2 | async-start | bytes 2621440 | tf_op jit(solution)/shard_map/all_gather | solution.py:40
  10.5 95.6 %reduce-scatter.3.cloned.1.call-start = ((), (), s32[]{:S(2)}) async-start(), calls=%async_computation.3 | async-start | bytes 5242880 | tf_op jit(solution)/shard_map/reduce_scatter | solution.py:46
  46.5 6.4 copy-start.2
  51.7 1.3 copy-start.12
  57.3 0.7 copy-start.6
  57.3 48.8 %copy-start = (bf16[1,2,128,2048]{3,2,1,0:T(8,128)(2,1)S(1)}, bf16[1,2,128,2048]{3,2,1,0:T(8,128)(2,1)}, u32[]{:S(2)}) copy-start(bf16[1,2,128,2048]{3,2,1,0:T(8,128)(2,1)} %param.15) | copy-start | bytes 3145732
  57.3 50.4 %copy-start.4 = (bf16[1,2,128,2048]{3,2,1,0:T(8,128)(2,1)S(1)}, bf16[1,2,128,2048]{3,2,1,0:T(8,128)(2,1)}, u32[]{:S(2)}) copy-start(bf16[1,2,128,2048]{3,2,1,0:T(8,128)(2,1)} %param.16) | copy-start | bytes 3145732
  57.3 52.3 %copy-start.7 = (f32[2048]{0:T(1024)S(1)}, f32[2048]{0:T(1024)}, u32[]{:S(2)}) copy-start(f32[2048]{0:T(1024)} %param.17) | copy-start | bytes 24580
  57.3 86.8 %all-gather.10.cloned.1.call-start = ((), (), s32[]{:S(2)}) async-start(), calls=%async_computation.4 | async-start | bytes 2621440 | tf_op jit(solution)/shard_map/all_gather | solution.py:128
  106.1 3.5 copy-start.1
  111.1 6.9 copy-start.8
  111.1 6.9 copy-start.9
  111.1 77.7 %all-gather.20.cloned.1.call-start = ((), (), s32[]{:S(2)}) async-start(), calls=%async_computation.9 | async-start | bytes 2621440 | tf_op jit(solution)/shard_map/all_gather | solution.py:40
  111.7 181.9 %all-gather.16.cloned.1.call-start = ((), (), s32[]{:S(2)}) async-start(), calls=%async_computation.7 | async-start | bytes 1064960 | tf_op jit(solution)/shard_map/all_gather | solution.py:104
  112.3 296.4 %all-gather.18.cloned.1.call-start = ((), (), s32[]{:S(2)}) async-start(), calls=%async_computation.8 | async-start | bytes 1064960 | tf_op jit(solution)/shard_map/all_gather | solution.py:106
  112.9 955.2 %all-reduce.4.cloned.1.call-start = ((), (), s32[]{:S(2)}) async-start(), calls=%async_computation.11 | async-start | bytes 4194304 | tf_op jit(solution)/shard_map/psum | solution.py:101
  116.3 1108.9 %all-gather.12.cloned.1.call-start = ((), (), s32[]{:S(2)}) async-start(), calls=%async_computation.5 | async-start | bytes 1064960 | tf_op jit(solution)/shard_map/all_gather | solution.py:103
  117.0 1222.8 %all-gather.14.cloned.1.call-start = ((), (), s32[]{:S(2)}) async-start(), calls=%async_computation.6 | async-start | bytes 1064960 | tf_op jit(solution)/shard_map/all_gather | solution.py:105
  117.7 1273.8 %reduce-scatter.5.cloned.1.call-start = ((), (), s32[]{:S(2)}) async-start(), calls=%async_computation.10 | async-start | bytes 5242880 | tf_op jit(solution)/shard_map/reduce_scatter | solution.py:46
  151.8 24.6 %copy-start.10 = (f32[1,896]{1,0:T(1,128)S(1)}, f32[1,896]{1,0:T(1,128)}, u32[]{:S(2)}) copy-start(f32[1,896]{1,0:T(1,128)} %param.24) | copy-start | bytes 10756
  151.8 24.6 %copy-start.11 = (f32[1,896]{1,0:T(1,128)S(1)}, f32[1,896]{1,0:T(1,128)}, u32[]{:S(2)}) copy-start(f32[1,896]{1,0:T(1,128)} %param.22) | copy-start | bytes 10756
  176.4 6.8 slice-start
  176.4 7.7 slice-start.1
  176.4 8.7 copy-start.3
  1068.1 271.7 %copy-start.5 = (f32[2048,128]{1,0:T(8,128)S(1)}, f32[2048,128]{1,0:T(8,128)}, u32[]{:S(2)}) copy-start(f32[2048,128]{1,0:T(8,128)} %get-tuple-element.14) | copy-start | bytes 3145732
Sparse Core Ops, SparseCore 0:
  10.6 35.8 all-gather.7
  57.4 48.6 reduce-scatter.2
  111.2 32.7 all-gather.9
  146.5 32.8 all-gather.19
  183.3 110.2 all-gather.15
  297.6 110.9 all-gather.17
  411.5 656.5 all-reduce.3
  1071.7 153.4 all-gather.11
  1228.8 110.9 all-gather.13
  1342.2 49.3 reduce-scatter.4
where the time goes:
time: 1400 us
  waiting for transfers between devices  1300 us (93%)
  matrix products  39.1 us (3%)
  other arithmetic  32.5 us (2%)
  between operations  16.3 us (1%)
    psum x1, waiting for transfers between devices, per_device(): total_up, total_down = lax.psum((start_up, start_down), 'rep')  659 us
    all_gather x1, waiting for transfers between devices, per_device(): lax.all_gather(anchor_up, 'rep', axis=0, tiled=True)  153 us
    all_gather x1, waiting for transfers between devices, per_device(): lax.all_gather(momentum_down, 'rep', axis=0, tiled=True)  115 us
    all_gather x1, waiting for transfers between devices, per_device(): lax.all_gather(momentum_up, 'rep', axis=0, tiled=True)  115 us
    reduce_scatter x2, waiting for transfers between devices, layer(): lax.psum_scatter(lax.dot_general(hidden, down_now, (((1,), (1,)), ((), ()...  95.8 us
    all_gather x1, waiting for transfers between devices, per_device(): lax.all_gather(anchor_down, 'rep', axis=0, tiled=True)  94.4 us
    all_gather x2, waiting for transfers between devices, layer(): normed_all = lax.all_gather(normed_low, 'fsdp', axis=0, tiled=True)  36 us
  transfers between devices with their start and end apart: 10, of which 9 were waited for; matrix products, arithmetic and copies ran while one was open for 4% of the time, Pallas kernels for 0%

commit v1 on v0

v1 whole, which is shorter than its diff:
```python
import functools
import math

import jax
import jax.numpy as jnp
from jax import lax
from jax.experimental import pallas as pl
from jax.experimental.pallas import tpu as pltpu
from jax.sharding import PartitionSpec as P

norm_epsilon = 1e-05
row_decay = 0.95
inner_rate = 0.05
weight_decay = 0.1
outer_rate = 0.7
outer_momentum = 0.9
mixing = 0.5

F32 = jnp.float32
BF16 = jnp.bfloat16
CHUNKS = 4


def mm(a, b):
    return jnp.dot(a, b, preferred_element_type=F32)


def mm_nt(a, b):
    return lax.dot_general(a, b, (((1,), (1,)), ((), ())), preferred_element_type=F32)


def mm_tn(a, b):
    return lax.dot_general(a, b, (((0,), (0,)), ((), ())), preferred_element_type=F32)


def pieces(extent, size):
    return [(s, min(size, extent - s)) for s in range(0, extent, size)]


def kernel(
    reps_z,
    reps_xy,
    frag,
    x_in,
    cot,
    mid_gain,
    out_gain,
    up_hbm,
    down_hbm,
    up_rows,
    up_cols,
    down_rows,
    down_cols,
    anchor_up,
    anchor_down,
    moment_up,
    moment_down,
    merged_up,
    merged_down,
    central_up,
    central_down,
    velocity_up,
    velocity_down,
    loss,
    up,
    down,
    x0,
    x1,
    db,
    slope,
    hid,
    dpre,
    part,
    from_sib0,
    from_sib1,
    to_peer0,
    to_peer1,
    from_peer0,
    from_peer1,
    grad_up,
    grad_down,
    block,
    from_z,
    sum_z,
    from_xy,
    central,
    rows_out,
    rows_in,
    cols_acc,
    load_sem,
    gather_sem,
    part_sem,
    rows_sem,
    z_sem,
    xy_sem,
    cxy_sem,
    cz_sem,
):
    width, units_here = up.shape
    tok = x_in.shape[1]
    shards = 4
    units = units_here * shards
    tokens = tok * shards
    reps = reps_z * reps_xy
    half = 2 * tok
    bw = block.shape[2]

    rep = lax.axis_index("rep")
    f = lax.axis_index("fsdp")
    z = rep // reps_xy
    xy = rep % reps_xy
    chip = f // 2
    core = f % 2
    sib = {"rep": rep, "fsdp": chip * 2 + (1 - core)}
    peer = {"rep": rep, "fsdp": (1 - chip) * 2 + core}
    diag = {"rep": rep, "fsdp": (1 - chip) * 2 + (1 - core)}

    def at_z(step):
        other = (z + step) % reps_z
        return other, {"rep": other * reps_xy + xy, "fsdp": f}

    def at_xy(step):
        other = (xy + step) % reps_xy
        return other, {"rep": z * reps_xy + other, "fsdp": f}

    sent = []

    def send(src, dst, sems, target):
        copy = pltpu.make_async_remote_copy(
            src_ref=src,
            dst_ref=dst,
            send_sem=sems.at[0],
            recv_sem=sems.at[1],
            device_id=target,
            device_id_type=pl.DeviceIdType.MESH,
        )
        copy.start()
        sent.append(copy)
        return copy

    load_up = pltpu.make_async_copy(up_hbm, up, load_sem.at[0])
    load_down = pltpu.make_async_copy(down_hbm, down, load_sem.at[1])
    load_up.start()
    load_down.start()

    barrier = pltpu.get_barrier_semaphore()
    partners = [sib, peer, diag]
    partners += [at_z(s)[1] for s in range(1, reps_z)]
    partners += [at_xy(s)[1] for s in range(1, reps_xy)]
    for partner in partners:
        pl.semaphore_signal(
            barrier, inc=1, device_id=partner, device_id_type=pl.DeviceIdType.MESH
        )

    rows_each = tok // CHUNKS

    def normalize_chunk(batch, dst, c):
        rows = slice(c * rows_each, (c + 1) * rows_each)
        v = x_in[batch, rows, :].astype(F32)
        factor = lax.rsqrt(jnp.mean(v * v, axis=-1, keepdims=True) + norm_epsilon)
        dst[rows, :] = (v * factor * mid_gain[...]).astype(BF16)

    def spread(buf, g, c):
        r = pl.ds(c * rows_each, rows_each)
        over = send(
            buf.at[r, :],
            buf.at[pl.ds(half + c * rows_each, rows_each), :],
            gather_sem.at[g, 1, c],
            peer,
        )
        near = send(
            buf.at[r, :],
            buf.at[pl.ds(tok + c * rows_each, rows_each), :],
            gather_sem.at[g, 0, c],
            sib,
        )
        return near, over

    def forward(buf, g, c, over):
        over.wait_recv()
        return send(
            buf.at[pl.ds(half + c * rows_each, rows_each), :],
            buf.at[pl.ds(half + tok + c * rows_each, rows_each), :],
            gather_sem.at[g, 2, c],
            sib,
        )

    for c in range(CHUNKS):
        normalize_chunk(0, x0, c)
    pl.semaphore_wait(barrier, len(partners))
    pairs0 = [spread(x0, 0, c) for c in range(CHUNKS)]

    strip = min(width, 256)
    chosen = [
        jnp.full((strip, bw), jnp.where(frag[0] == k, 1.0, 0.0), F32).astype(BF16)
        for k in range(units_here // bw)
    ]

    def fragment_rows(weight, k):
        rows = pl.ds(k, strip)
        picked = weight[rows, 0:bw] * chosen[0]
        for n in range(1, units_here // bw):
            picked = picked + weight[rows, n * bw : (n + 1) * bw] * chosen[n]
        return picked

    load_up.wait()
    load_down.wait()
    for k in range(0, width, strip):
        block[0, k : k + strip, :] = fragment_rows(up, k)
        block[1, k : k + strip, :] = fragment_rows(down, k)
    span_z = width // reps_z
    span = width // reps
    z_copies = []
    for s in range(1, reps_z):
        other, target = at_z(s)
        z_copies.append(
            send(
                block.at[:, pl.ds(other * span_z, span_z), :],
                from_z.at[s - 1],
                z_sem.at[s - 1],
                target,
            )
        )

    def sum_over_z():
        for w in range(2):
            total = block[w, pl.ds(z * span_z, span_z), :].astype(F32)
            for s in range(1, reps_z):
                if w == 0:
                    z_copies[s - 1].wait_recv()
                total = total + from_z[s - 1, w].astype(F32)
            sum_z[w] = total
        copies = []
        for s in range(1, reps_xy):
            other, target = at_xy(s)
            copies.append(
                send(
                    sum_z.at[:, pl.ds(other * span, span), :],
                    from_xy.at[s - 1],
                    xy_sem.at[s - 1],
                    target,
                )
            )
        return copies

    def outer_step(copies):
        for copy in copies:
            copy.wait_recv()
        mine = pl.ds(rep * span, span)
        for w, (anchor, moment, cent_out, vel_out) in enumerate(
            (
                (anchor_up, moment_up, central_up, velocity_up),
                (anchor_down, moment_down, central_down, velocity_down),
            )
        ):
            total = sum_z[w, pl.ds(xy * span, span), :]
            for s in range(1, reps_xy):
                total = total + from_xy[s - 1, w]
            drift = anchor[...] - total / reps
            velocity = outer_momentum * moment[...] + drift
            cent = anchor[...] - outer_rate * (drift + outer_momentum * velocity)
            vel_out[...] = velocity
            cent_out[...] = cent
            central[w, mine, :] = cent
        out = []
        for s in range(1, reps_xy):
            _, target = at_xy(s)
            out.append(
                send(central.at[:, mine, :], central.at[:, mine, :], cxy_sem.at[s - 1], target)
            )
        return out

    def gather_over_z(copies):
        for copy in copies:
            copy.wait_recv()
        slab = pl.ds(z * span_z, span_z)
        out = []
        for s in range(1, reps_z):
            _, target = at_z(s)
            out.append(
                send(central.at[:, slab, :], central.at[:, slab, :], cz_sem.at[s - 1], target)
            )
        return out

    def hidden_of(buf, lo, count, keep_slope):
        rows = slice(lo, lo + count)
        for n, size in pieces(units_here, 256):
            pre = mm(buf[rows, :], up[:, n : n + size]) * (1.0 / math.sqrt(width))
            sig = jax.nn.sigmoid(pre)
            hid[rows, n : n + size] = (pre * sig).astype(BF16)
            if keep_slope:
                slope[rows, n : n + size] = (
                    sig * (1 + pre * (1 - sig)) * (1.0 / math.sqrt(width))
                )

    feats = width // CHUNKS

    def branch_of(lo, count, j):
        part[lo : lo + count, j * feats : (j + 1) * feats] = mm_nt(
            hid[lo : lo + count, :], down[j * feats : (j + 1) * feats, :]
        )

    def sib_send(b, which, j, dst):
        lo = tok + which * half
        cols = pl.ds(j * feats, feats)
        return send(
            part.at[pl.ds(lo, tok), cols],
            dst.at[which, :, cols],
            part_sem.at[b, which, j],
            sib,
        )

    def peer_send(b, j, copy, src_sib, staged, dst):
        copy.wait_recv()
        cols = slice(j * feats, (j + 1) * feats)
        staged[:, cols] = (part[half : half + tok, cols] + src_sib[1, :, cols]).astype(BF16)
        ds = pl.ds(j * feats, feats)
        return send(staged.at[:, ds], dst.at[:, ds], part_sem.at[b, 2, j], peer)

    def lanes_of(column_vector):
        wide = jnp.broadcast_to(column_vector, (tok, 128))
        return jnp.transpose(wide)[0:1, :]

    for near, _ in pairs0:
        near.wait_recv()
    hidden_of(x0, 0, half, True)
    diag0 = []
    near_part0 = []
    for j in range(CHUNKS):
        branch_of(0, half, j)
        near_part0.append(sib_send(0, 0, j, from_sib0))
        diag0.append(forward(x0, 0, j, pairs0[j][1]))
    for copy in diag0:
        copy.wait_recv()
    hidden_of(x0, half, half, True)
    far_part0 = []
    over_part0 = []
    for j in range(CHUNKS):
        branch_of(half, half, j)
        far_part0.append(sib_send(0, 1, j, from_sib0))
        if j:
            over_part0.append(
                peer_send(0, j - 1, far_part0[j - 1], from_sib0, to_peer0, from_peer0)
            )
    over_part0.append(
        peer_send(0, CHUNKS - 1, far_part0[-1], from_sib0, to_peer0, from_peer0)
    )
    for c in range(CHUNKS):
        normalize_chunk(1, x1, c)
    xy_copies = sum_over_z()
    for copy in near_part0 + over_part0:
        copy.wait_recv()

    def output_of(b, c, src_sib, src_peer):
        rows = slice(c * rows_each, (c + 1) * rows_each)
        branch = part[rows, :] + src_sib[0, rows, :] + src_peer[rows, :].astype(F32)
        output = x_in[b, rows, :].astype(F32) + branch * (1.0 / math.sqrt(units))
        q = lax.rsqrt(jnp.mean(output * output, axis=-1, keepdims=True) + norm_epsilon)
        c_gain = cot[b, rows, :].astype(F32) * out_gain[...]
        dotted = jnp.sum(c_gain * output, axis=-1, keepdims=True)
        return output, q, c_gain, dotted

    def token_losses(columns):
        return lanes_of(jnp.concatenate(columns, axis=0))

    pairs_d = []
    losses = []
    for c in range(CHUNKS):
        output, q, c_gain, dotted = output_of(0, c, from_sib0, from_peer0)
        losses.append(dotted * q)
        g = c_gain * (1.0 / tokens)
        doutput = q * g - output * (q * q * q * (dotted * (1.0 / (tokens * width))))
        db[c * rows_each : (c + 1) * rows_each, :] = (
            doutput * (1.0 / math.sqrt(units))
        ).astype(BF16)
        pairs_d.append(spread(db, 1, c))
    loss[0:1, :] = token_losses(losses)
    cxy_copies = outer_step(xy_copies)

    def dpre_of(lo, count):
        rows = slice(lo, lo + count)
        for n, size in pieces(units_here, 256):
            dh = mm(db[rows, :], down[:, n : n + size])
            dpre[rows, n : n + size] = (dh * slope[rows, n : n + size]).astype(BF16)

    step = 256
    n_steps = width // step

    def first_half(dst, left, right):
        def body(i, carry):
            k = pl.multiple_of(i * step, step)
            dst[pl.ds(k, step), :] = mm_tn(left[0:half, pl.ds(k, step)], right[0:half, :])
            return carry

        lax.fori_loop(0, n_steps, body, 0)

    def second_half(w, dst, left, right):
        cols_acc[w] = jnp.zeros((1, units_here), F32)

        def body(i, carry):
            k = pl.multiple_of(i * step, step)
            g = dst[pl.ds(k, step), :] + mm_tn(
                left[half : 2 * half, pl.ds(k, step)], right[half : 2 * half, :]
            )
            dst[pl.ds(k, step), :] = g
            sq = g * g
            cols_acc[w] += jnp.sum(sq, axis=0, keepdims=True)
            lanes = sq[:, 0:128]
            for s in range(128, units_here, 128):
                lanes = lanes + sq[:, s : s + 128]
            rows_out[w, :, pl.ds(k, step)] = jnp.sum(
                jnp.transpose(lanes), axis=0, keepdims=True
            )
            return carry

        lax.fori_loop(0, n_steps, body, 0)
        return [
            send(rows_out.at[w], rows_in.at[w, i], rows_sem.at[w, i], target)
            for i, target in enumerate((sib, peer, diag))
        ]

    for near, _ in pairs_d:
        near.wait_recv()
    dpre_of(0, half)
    diag_d = [forward(db, 1, 0, pairs_d[0][1])]
    first_half(grad_up, x0, dpre)
    diag_d.append(forward(db, 1, 1, pairs_d[1][1]))
    first_half(grad_down, db, hid)
    for c in range(2, CHUNKS):
        diag_d.append(forward(db, 1, c, pairs_d[c][1]))
    cz_copies = gather_over_z(cxy_copies)
    for copy in diag_d:
        copy.wait_recv()
    pairs1 = [spread(x1, 2, c) for c in range(CHUNKS)]
    dpre_of(half, half)
    rows_up_copies = second_half(0, grad_up, x0, dpre)
    diag1 = [forward(x1, 2, c, pairs1[c][1]) for c in range(2)]
    rows_down_copies = second_half(1, grad_down, db, hid)

    def factors(w, copies, rows_ref, cols_ref):
        for copy in copies:
            copy.wait_recv()
        total = rows_out[w] + rows_in[w, 0] + rows_in[w, 1] + rows_in[w, 2]
        rows2 = row_decay * rows_ref[...] + ((1 - row_decay) / units) * total
        cols2 = row_decay * cols_ref[...] + ((1 - row_decay) / width) * cols_acc[w]
        mean = jnp.mean(rows2, axis=-1, keepdims=True)
        rows_in[w, 0] = lax.rsqrt(rows2) * inner_rate
        cols_acc[w] = lax.rsqrt(cols2 / mean)

    def update(w, weight, grad, k, size):
        scale = jnp.transpose(
            jnp.broadcast_to(rows_in[w, 0, :, pl.ds(k, size)], (128, size))
        )
        for s in range(0, units_here, 128):
            move = grad[pl.ds(k, size), s : s + 128] * scale * cols_acc[w, :, s : s + 128]
            old = weight[pl.ds(k, size), s : s + 128].astype(F32)
            weight[pl.ds(k, size), s : s + 128] = (
                old * (1 - inner_rate * weight_decay) - move
            ).astype(BF16)

    def update_all(w, weight, grad):
        def body(i, carry):
            update(w, weight, grad, pl.multiple_of(i * step, step), step)
            return carry

        lax.fori_loop(0, n_steps, body, 0)

    factors(0, rows_up_copies, up_rows, up_cols)
    update_all(0, up, grad_up)
    diag1 += [forward(x1, 2, c, pairs1[c][1]) for c in range(2, CHUNKS)]
    for (near, _), far in zip(pairs1, diag1):
        near.wait_recv()
        far.wait_recv()
    hidden_of(x1, 0, 2 * half, False)
    factors(1, rows_down_copies, down_rows, down_cols)
    for copy in near_part0 + far_part0:
        copy.wait_send()
        sent[:] = [other for other in sent if other is not copy]
    near_part1 = []
    far_part1 = []
    over_part1 = []
    for j in range(CHUNKS):
        for k, size in pieces(feats, step):
            update(1, down, grad_down, j * feats + k, size)
        branch_of(0, 2 * half, j)
        far_part1.append(sib_send(1, 1, j, from_sib1))
        near_part1.append(sib_send(1, 0, j, from_sib1))
        if j:
            over_part1.append(
                peer_send(1, j - 1, far_part1[j - 1], from_sib1, to_peer1, from_peer1)
            )
    over_part1.append(
        peer_send(1, CHUNKS - 1, far_part1[-1], from_sib1, to_peer1, from_peer1)
    )

    for copy in cz_copies:
        copy.wait_recv()
    for k in range(0, width, strip):
        for w, (weight, merged) in enumerate(((up, merged_up), (down, merged_down))):
            merged[k : k + strip, :] = (
                mixing * fragment_rows(weight, k).astype(F32)
                + (1 - mixing) * central[w, k : k + strip, :]
            ).astype(BF16)

    for copy in near_part1 + over_part1:
        copy.wait_recv()
    losses = []
    for c in range(CHUNKS):
        _, q, _, dotted = output_of(1, c, from_sib1, from_peer1)
        losses.append(dotted * q)
    loss[1:2, :] = token_losses(losses)
    for copy in sent:
        copy.wait_send()


def per_device(reps_z, reps_xy, inputs, cotangent, mid_gain, out_gain, up_weight, down_weight,
               up_rows, up_cols, down_rows, down_cols, anchor_up, anchor_down,
               momentum_up, momentum_down, fragment):
    _, _, tok, width = inputs.shape
    units_here = up_weight.shape[2]
    span, bw = anchor_up.shape
    reps = reps_z * reps_xy
    tokens = 4 * tok
    vmem = pl.BlockSpec(memory_space=pltpu.VMEM)
    hbm = pl.BlockSpec(memory_space=pl.ANY)
    smem = pl.BlockSpec(memory_space=pltpu.SMEM)
    flops = 7 * 2 * tokens * width * units_here
    results = pl.pallas_call(
        functools.partial(kernel, reps_z, reps_xy),
        out_shape=(
            jax.ShapeDtypeStruct((width, bw), BF16),
            jax.ShapeDtypeStruct((width, bw), BF16),
            jax.ShapeDtypeStruct((span, bw), F32),
            jax.ShapeDtypeStruct((span, bw), F32),
            jax.ShapeDtypeStruct((span, bw), F32),
            jax.ShapeDtypeStruct((span, bw), F32),
            jax.ShapeDtypeStruct((2, tok), F32),
        ),
        in_specs=[smem, vmem, vmem, vmem, vmem, hbm, hbm] + [vmem] * 8,
        out_specs=tuple([vmem] * 7),
        scratch_shapes=[
            pltpu.VMEM((width, units_here), BF16),
            pltpu.VMEM((width, units_here), BF16),
            pltpu.VMEM((tokens, width), BF16),
            pltpu.VMEM((tokens, width), BF16),
            pltpu.VMEM((tokens, width), BF16),
            pltpu.VMEM((tokens, units_here), F32),
            pltpu.VMEM((tokens, units_here), BF16),
            pltpu.VMEM((tokens, units_here), BF16),
            pltpu.VMEM((tokens, width), F32),
            pltpu.VMEM((2, tok, width), F32),
            pltpu.VMEM((2, tok, width), F32),
            pltpu.VMEM((tok, width), BF16),
            pltpu.VMEM((tok, width), BF16),
            pltpu.VMEM((tok, width), BF16),
            pltpu.VMEM((tok, width), BF16),
            pltpu.VMEM((width, units_here), F32),
            pltpu.VMEM((width, units_here), F32),
            pltpu.VMEM((2, width, bw), BF16),
            pltpu.VMEM((reps_z - 1, 2, width // reps_z, bw), BF16),
            pltpu.VMEM((2, width // reps_z, bw), F32),
            pltpu.VMEM((reps_xy - 1, 2, span, bw), F32),
            pltpu.VMEM((2, width, bw), F32),
            pltpu.VMEM((2, 1, width), F32),
            pltpu.VMEM((2, 3, 1, width), F32),
            pltpu.VMEM((2, 1, units_here), F32),
            pltpu.SemaphoreType.DMA((2,)),
            pltpu.SemaphoreType.DMA((3, 3, CHUNKS, 2)),
            pltpu.SemaphoreType.DMA((2, 3, CHUNKS, 2)),
            pltpu.SemaphoreType.DMA((2, 3, 2)),
            pltpu.SemaphoreType.DMA((reps_z - 1, 2)),
            pltpu.SemaphoreType.DMA((reps_xy - 1, 2)),
            pltpu.SemaphoreType.DMA((reps_xy - 1, 2)),
            pltpu.SemaphoreType.DMA((reps_z - 1, 2)),
        ],
        compiler_params=pltpu.CompilerParams(
            collective_id=0,
            has_side_effects=True,
            vmem_limit_bytes=62 * 1024 * 1024,
        ),
        cost_estimate=pl.CostEstimate(
            flops=flops, bytes_accessed=10_000_000, transcendentals=0
        ),
        name="window",
    )(
        fragment,
        inputs[0],
        cotangent[0],
        mid_gain[None],
        out_gain[None],
        up_weight[0],
        down_weight[0],
        up_rows,
        up_cols,
        down_rows,
        down_cols,
        anchor_up,
        anchor_down,
        momentum_up,
        momentum_down,
    )
    merged_up, merged_down, c_up, c_down, v_up, v_down, loss = results
    return merged_up[None], merged_down[None], c_up, c_down, v_up, v_down, loss[None]


def solution(mesh):
    reps = mesh.shape["rep"]
    reps_xy = 8 if reps % 8 == 0 and reps > 8 else 2
    reps_z = reps // reps_xy
    placed = (
        P("rep", None, "fsdp", None),
        P("rep", None, "fsdp", None),
        P(),
        P(),
        P("rep", None, "fsdp"),
        P("rep", None, "fsdp"),
        P("rep", None),
        P("rep", "fsdp"),
        P("rep", None),
        P("rep", "fsdp"),
        P("rep", "fsdp"),
        P("rep", "fsdp"),
        P("rep", "fsdp"),
        P("rep", "fsdp"),
        P(),
    )
    return jax.shard_map(
        functools.partial(per_device, reps_z, reps_xy),
        mesh=mesh,
        in_specs=placed,
        out_specs=(
            P("rep", None, "fsdp"),
            P("rep", None, "fsdp"),
            P("rep", "fsdp"),
            P("rep", "fsdp"),
            P("rep", "fsdp"),
            P("rep", "fsdp"),
            P("rep", None, "fsdp"),
        ),
        check_vma=False,
    )
```

time: 1400 us -> 122 us (0.09)
  the two profiles are of different devices: /device:TPU:1 before, /device:TPU:30 now
where the time goes in v1:
time: 122 us; the launch traced here: 121 us
  Pallas kernels  110 us (90%)
  local copies, waits for them, and re-layouts  10.3 us (8%)
  between operations  1.3 us (1%)
    pallas_call x1, Pallas kernels, per_device(): pl.pallas_call(functools.partial(kernel, reps_z, reps_xy), out_shape=(jax...  110 us
    unnamed x7, local copies, waits for them, and re-layouts  10.3 us

profile of v1, /device:TPU:30, one launch (start us, length us, event | category | flops | bytes accessed | tf_op | source)
XLA Modules:
  0.0 121.1 jit_solution(16878293471018192226)
XLA Ops:
  1.3 109.5 %window.1 = (bf16[2048,128]{1,0:T(8,128)(2,1)}, bf16[2048,128]{1,0:T(8,128)(2,1)}, f32[32,128]{1,0:T(8,128)}, f32[32,128]{1,0:T(8,128)}, f32[32,128]{1,0:T(8,128)}, /*index=5*/f32[32,128]{1,0:T(8,128)}, f32[2,128]{1,0:T(2,128)}) custom-call(s32[1]{0:T(128)S(6)} %copy.29.frag, bf16[2,128,2048]{2,1,0:T(8,128)(2,1)} %bitcast.14, ...), custom_call_target="tpu_custom_call" | custom-call | flops 13153337344 | bytes 10000000 | tf_op jit(solution)/shard_map/window/pallas_call | solution.py:528
  110.8 1.9 %copy.30 = bf16[1,2048,128]{2,1,0:T(8,128)(2,1)} copy(bf16[1,2048,128]{2,1,0:T(8,128)(2,1)} %bitcast.10) | data formatting | bytes 1048576
  112.7 1.9 %copy.31 = bf16[1,2048,128]{2,1,0:T(8,128)(2,1)} copy(bf16[1,2048,128]{2,1,0:T(8,128)(2,1)} %bitcast.9) | data formatting | bytes 1048576
  114.5 1.3 %copy.32 = f32[32,128]{1,0:T(8,128)} copy(f32[32,128]{1,0:T(8,128)} %get-tuple-element.30) | data formatting | bytes 32768
  115.9 1.3 %copy.33 = f32[32,128]{1,0:T(8,128)} copy(f32[32,128]{1,0:T(8,128)} %get-tuple-element.31) | data formatting | bytes 32768
  117.2 1.3 %copy.34 = f32[32,128]{1,0:T(8,128)} copy(f32[32,128]{1,0:T(8,128)} %get-tuple-element.32) | data formatting | bytes 32768
  118.5 1.3 %copy.35 = f32[32,128]{1,0:T(8,128)} copy(f32[32,128]{1,0:T(8,128)} %get-tuple-element.33) | data formatting | bytes 32768
  119.8 1.2 %copy.36 = f32[1,2,128]{2,1,0:T(2,128)} copy(f32[1,2,128]{2,1,0:T(2,128)} %bitcast.11) | data formatting | bytes 2048

commit v2 on v1

--- a/solution.py
+++ b/solution.py
@@ -39,7 +39,7 @@
 
 def kernel(
     reps_z,
-    reps_xy,
+    reps_y,
     frag,
     x_in,
     cot,
@@ -80,9 +80,14 @@
     grad_up,
     grad_down,
     block,
-    from_z,
-    sum_z,
-    from_xy,
+    up_from_y,
+    up_y,
+    up_from_z,
+    down_from_z,
+    down_z,
+    down_from_y,
+    pair,
+    from_x,
     central,
     rows_out,
     rows_in,
@@ -91,37 +96,38 @@
     gather_sem,
     part_sem,
     rows_sem,
-    z_sem,
-    xy_sem,
-    cxy_sem,
-    cz_sem,
+    a_sem,
+    b_sem,
+    c_sem,
+    e_sem,
+    f_sem,
 ):
     width, units_here = up.shape
     tok = x_in.shape[1]
     shards = 4
     units = units_here * shards
     tokens = tok * shards
-    reps = reps_z * reps_xy
+    reps = reps_z * 2 * reps_y
     half = 2 * tok
-    bw = block.shape[2]
+    bw = block.shape[4]
 
     rep = lax.axis_index("rep")
     f = lax.axis_index("fsdp")
-    z = rep // reps_xy
-    xy = rep % reps_xy
+    z = rep // (2 * reps_y)
+    xh = rep // reps_y % 2
+    y = rep % reps_y
     chip = f // 2
     core = f % 2
     sib = {"rep": rep, "fsdp": chip * 2 + (1 - core)}
     peer = {"rep": rep, "fsdp": (1 - chip) * 2 + core}
     diag = {"rep": rep, "fsdp": (1 - chip) * 2 + (1 - core)}
 
-    def at_z(step):
-        other = (z + step) % reps_z
-        return other, {"rep": other * reps_xy + xy, "fsdp": f}
-
-    def at_xy(step):
-        other = (xy + step) % reps_xy
-        return other, {"rep": z * reps_xy + other, "fsdp": f}
+    def device(z_, xh_, y_):
+        return {"rep": (z_ * 2 + xh_) * reps_y + y_, "fsdp": f}
+
+    across = device(z, 1 - xh, y)
+    others_z = [(z + s) % reps_z for s in range(1, reps_z)]
+    others_y = [(y + s) % reps_y for s in range(1, reps_y)]
 
     sent = []
 
@@ -145,8 +151,9 @@
 
     barrier = pltpu.get_barrier_semaphore()
     partners = [sib, peer, diag]
-    partners += [at_z(s)[1] for s in range(1, reps_z)]
-    partners += [at_xy(s)[1] for s in range(1, reps_xy)]
+    partners += [device(o, xh, y) for o in others_z]
+    partners += [device(z, xh, o) for o in others_y]
+    partners += [across]
     for partner in partners:
         pl.semaphore_signal(
             barrier, inc=1, device_id=partner, device_id_type=pl.DeviceIdType.MESH
@@ -190,97 +197,133 @@
     pl.semaphore_wait(barrier, len(partners))
     pairs0 = [spread(x0, 0, c) for c in range(CHUNKS)]
 
-    strip = min(width, 256)
-    chosen = [
-        jnp.full((strip, bw), jnp.where(frag[0] == k, 1.0, 0.0), F32).astype(BF16)
-        for k in range(units_here // bw)
-    ]
-
-    def fragment_rows(weight, k):
+    chosen = [jnp.where(frag[0] == k, 1.0, 0.0) for k in range(units_here // bw)]
+
+    def fragment_rows(weight, k, strip):
         rows = pl.ds(k, strip)
-        picked = weight[rows, 0:bw] * chosen[0]
-        for n in range(1, units_here // bw):
-            picked = picked + weight[rows, n * bw : (n + 1) * bw] * chosen[n]
+        picked = None
+        for n, one in enumerate(chosen):
+            term = weight[rows, n * bw : (n + 1) * bw] * jnp.full(
+                (strip, bw), one, F32
+            ).astype(BF16)
+            picked = term if picked is None else picked + term
         return picked
 
     load_up.wait()
     load_down.wait()
-    for k in range(0, width, strip):
-        block[0, k : k + strip, :] = fragment_rows(up, k)
-        block[1, k : k + strip, :] = fragment_rows(down, k)
-    span_z = width // reps_z
     span = width // reps
-    z_copies = []
-    for s in range(1, reps_z):
-        other, target = at_z(s)
-        z_copies.append(
+    slab = reps_y * span
+    for k in range(0, width, slab):
+        block[0, k // slab] = fragment_rows(up, k, slab).reshape(reps_y, span, bw)
+        block[1, k // slab] = fragment_rows(down, k, slab).reshape(reps_y, span, bw)
+    here = pl.ds(z * 2, 2)
+
+    def spread_blocks():
+        over_y = [
+            send(block.at[0, :, o], up_from_y.at[i], a_sem.at[0, i], device(z, xh, o))
+            for i, o in enumerate(others_y)
+        ]
+        over_z = [
             send(
-                block.at[:, pl.ds(other * span_z, span_z), :],
-                from_z.at[s - 1],
-                z_sem.at[s - 1],
-                target,
+                block.at[1, pl.ds(o * 2, 2)],
+                down_from_z.at[i],
+                a_sem.at[1, i],
+                device(o, xh, y),
             )
-        )
-
-    def sum_over_z():
-        for w in range(2):
-            total = block[w, pl.ds(z * span_z, span_z), :].astype(F32)
-            for s in range(1, reps_z):
-                if w == 0:
-                    z_copies[s - 1].wait_recv()
-                total = total + from_z[s - 1, w].astype(F32)
-            sum_z[w] = total
-        copies = []
-        for s in range(1, reps_xy):
-            other, target = at_xy(s)
-            copies.append(
-                send(
-                    sum_z.at[:, pl.ds(other * span, span), :],
-                    from_xy.at[s - 1],
-                    xy_sem.at[s - 1],
-                    target,
-                )
+            for i, o in enumerate(others_z)
+        ]
+        return over_y, over_z
+
+    def sum_once(copies):
+        over_y, over_z = copies
+        for copy in over_y:
+            copy.wait_recv()
+        total = block[0, :, y].astype(F32)
+        for i in range(reps_y - 1):
+            total = total + up_from_y[i].astype(F32)
+        up_y[...] = total
+        up_z_copies = [
+            send(
+                up_y.at[pl.ds(o * 2, 2)], up_from_z.at[i], b_sem.at[0, i], device(o, xh, y)
             )
-        return copies
-
-    def outer_step(copies):
-        for copy in copies:
+            for i, o in enumerate(others_z)
+        ]
+        for copy in over_z:
             copy.wait_recv()
-        mine = pl.ds(rep * span, span)
+        total = block[1, here].astype(F32)
+        for i in range(reps_z - 1):
+            total = total + down_from_z[i].astype(F32)
+        down_z[...] = total
+        down_y_copies = [
+            send(down_z.at[:, o], down_from_y.at[i], b_sem.at[1, i], device(z, xh, o))
+            for i, o in enumerate(others_y)
+        ]
+        return up_z_copies, down_y_copies
+
+    def sum_twice(copies):
+        for copy in copies[0] + copies[1]:
+            copy.wait_recv()
+        total = up_y[here]
+        for i in range(reps_z - 1):
+            total = total + up_from_z[i]
+        pair[:, 0] = total
+        total = down_z[:, y]
+        for i in range(reps_y - 1):
+            total = total + down_from_y[i]
+        pair[:, 1] = total
+        return send(pair.at[1 - xh], from_x, c_sem.at[0], across)
+
+    def outer_step(copy):
+        copy.wait_recv()
         for w, (anchor, moment, cent_out, vel_out) in enumerate(
             (
                 (anchor_up, moment_up, central_up, velocity_up),
                 (anchor_down, moment_down, central_down, velocity_down),
             )
         ):
-            total = sum_z[w, pl.ds(xy * span, span), :]
-            for s in range(1, reps_xy):
-                total = total + from_xy[s - 1, w]
+            total = pair[xh, w] + from_x[w]
             drift = anchor[...] - total / reps
             velocity = outer_momentum * moment[...] + drift
             cent = anchor[...] - outer_rate * (drift + outer_momentum * velocity)
             vel_out[...] = velocity
             cent_out[...] = cent
-            central[w, mine, :] = cent
-        out = []
-        for s in range(1, reps_xy):
-            _, target = at_xy(s)
-            out.append(
-                send(central.at[:, mine, :], central.at[:, mine, :], cxy_sem.at[s - 1], target)
-            )
+            central[w, z * 2 + xh, y] = cent
+        mine = central.at[:, z * 2 + xh, y]
+        return send(mine, mine, c_sem.at[1], across)
+
+    def gather_once(copy):
+        copy.wait_recv()
+        up_here = central.at[0, here, y]
+        down_here = central.at[1, here, y]
+        over_z = [
+            send(up_here, up_here, e_sem.at[0, i], device(o, xh, y))
+            for i, o in enumerate(others_z)
+        ]
+        over_y = [
+            send(down_here, down_here, e_sem.at[1, i], device(z, xh, o))
+            for i, o in enumerate(others_y)
+        ]
+        return over_z, over_y
+
+    def gather_twice(copies):
+        over_z, over_y = copies
+        for copy in over_y:
+            copy.wait_recv()
+        down_here = central.at[1, here]
+        out = [
+            send(down_here, down_here, f_sem.at[1, i], device(o, xh, y))
+            for i, o in enumerate(others_z)
+        ]
+        for copy in over_z:
+            copy.wait_recv()
+        up_here = central.at[0, :, y]
+        out += [
+            send(up_here, up_here, f_sem.at[0, i], device(z, xh, o))
+            for i, o in enumerate(others_y)
+        ]
         return out
 
-    def gather_over_z(copies):
-        for copy in copies:
-            copy.wait_recv()
-        slab = pl.ds(z * span_z, span_z)
-        out = []
-        for s in range(1, reps_z):
-            _, target = at_z(s)
-            out.append(
-                send(central.at[:, slab, :], central.at[:, slab, :], cz_sem.at[s - 1], target)
-            )
-        return out
+    block_copies = spread_blocks()
 
     def hidden_of(buf, lo, count, keep_slope):
         rows = slice(lo, lo + count)
@@ -347,7 +390,7 @@
     )
     for c in range(CHUNKS):
         normalize_chunk(1, x1, c)
-    xy_copies = sum_over_z()
+    b_copies = sum_once(block_copies)
     for copy in near_part0 + over_part0:
         copy.wait_recv()
 
@@ -375,7 +418,7 @@
         ).astype(BF16)
         pairs_d.append(spread(db, 1, c))
     loss[0:1, :] = token_losses(losses)
-    cxy_copies = outer_step(xy_copies)
+    c_copy = sum_twice(b_copies)
 
     def dpre_of(lo, count):
         rows = slice(lo, lo + count)
@@ -428,14 +471,16 @@
     first_half(grad_down, db, hid)
     for c in range(2, CHUNKS):
         diag_d.append(forward(db, 1, c, pairs_d[c][1]))
-    cz_copies = gather_over_z(cxy_copies)
+    d_copy = outer_step(c_copy)
     for copy in diag_d:
         copy.wait_recv()
     pairs1 = [spread(x1, 2, c) for c in range(CHUNKS)]
     dpre_of(half, half)
     rows_up_copies = second_half(0, grad_up, x0, dpre)
+    e_copies = gather_once(d_copy)
     diag1 = [forward(x1, 2, c, pairs1[c][1]) for c in range(2)]
     rows_down_copies = second_half(1, grad_down, db, hid)
+    f_copies = gather_twice(e_copies)
 
     def factors(w, copies, rows_ref, cols_ref):
         for copy in copies:
@@ -493,13 +538,13 @@
         peer_send(1, CHUNKS - 1, far_part1[-1], from_sib1, to_peer1, from_peer1)
     )
 
-    for copy in cz_copies:
+    for copy in f_copies:
         copy.wait_recv()
-    for k in range(0, width, strip):
+    for k in range(0, width, slab):
         for w, (weight, merged) in enumerate(((up, merged_up), (down, merged_down))):
-            merged[k : k + strip, :] = (
-                mixing * fragment_rows(weight, k).astype(F32)
-                + (1 - mixing) * central[w, k : k + strip, :]
+            merged[k : k + slab, :] = (
+                mixing * fragment_rows(weight, k, slab).astype(F32)
+                + (1 - mixing) * central[w, k // slab].reshape(slab, bw)
             ).astype(BF16)
 
     for copy in near_part1 + over_part1:
@@ -513,20 +558,25 @@
         copy.wait_send()
 
 
-def per_device(reps_z, reps_xy, inputs, cotangent, mid_gain, out_gain, up_weight, down_weight,
+def hand_over(n, *refs):
+    for i in range(n):
+        refs[n + i][...] = refs[i][...]
+
+
+def per_device(reps_z, reps_y, inputs, cotangent, mid_gain, out_gain, up_weight, down_weight,
                up_rows, up_cols, down_rows, down_cols, anchor_up, anchor_down,
                momentum_up, momentum_down, fragment):
     _, _, tok, width = inputs.shape
     units_here = up_weight.shape[2]
     span, bw = anchor_up.shape
-    reps = reps_z * reps_xy
+    reps = reps_z * 2 * reps_y
     tokens = 4 * tok
     vmem = pl.BlockSpec(memory_space=pltpu.VMEM)
     hbm = pl.BlockSpec(memory_space=pl.ANY)
     smem = pl.BlockSpec(memory_space=pltpu.SMEM)
     flops = 7 * 2 * tokens * width * units_here
     results = pl.pallas_call(
-        functools.partial(kernel, reps_z, reps_xy),
+        functools.partial(kernel, reps_z, reps_y),
         out_shape=(
             jax.ShapeDtypeStruct((width, bw), BF16),
             jax.ShapeDtypeStruct((width, bw), BF16),
@@ -556,11 +606,16 @@
             pltpu.VMEM((tok, width), BF16),
             pltpu.VMEM((width, units_here), F32),
             pltpu.VMEM((width, units_here), F32),
-            pltpu.VMEM((2, width, bw), BF16),
-            pltpu.VMEM((reps_z - 1, 2, width // reps_z, bw), BF16),
-            pltpu.VMEM((2, width // reps_z, bw), F32),
-            pltpu.VMEM((reps_xy - 1, 2, span, bw), F32),
-            pltpu.VMEM((2, width, bw), F32),
+            pltpu.VMEM((2, 2 * reps_z, reps_y, span, bw), BF16),
+            pltpu.VMEM((reps_y - 1, 2 * reps_z, span, bw), BF16),
+            pltpu.VMEM((2 * reps_z, span, bw), F32),
+            pltpu.VMEM((reps_z - 1, 2, span, bw), F32),
+            pltpu.VMEM((reps_z - 1, 2, reps_y, span, bw), BF16),
+            pltpu.VMEM((2, reps_y, span, bw), F32),
+            pltpu.VMEM((reps_y - 1, 2, span, bw), F32),
+            pltpu.VMEM((2, 2, span, bw), F32),
+            pltpu.VMEM((2, span, bw), F32),
+            pltpu.VMEM((2, 2 * reps_z, reps_y, span, bw), F32),
             pltpu.VMEM((2, 1, width), F32),
             pltpu.VMEM((2, 3, 1, width), F32),
             pltpu.VMEM((2, 1, units_here), F32),
@@ -568,10 +623,11 @@
             pltpu.SemaphoreType.DMA((3, 3, CHUNKS, 2)),
             pltpu.SemaphoreType.DMA((2, 3, CHUNKS, 2)),
             pltpu.SemaphoreType.DMA((2, 3, 2)),
-            pltpu.SemaphoreType.DMA((reps_z - 1, 2)),
-            pltpu.SemaphoreType.DMA((reps_xy - 1, 2)),
-            pltpu.SemaphoreType.DMA((reps_xy - 1, 2)),
-            pltpu.SemaphoreType.DMA((reps_z - 1, 2)),
+            pltpu.SemaphoreType.DMA((2, max(reps_y, reps_z) - 1, 2)),
+            pltpu.SemaphoreType.DMA((2, max(reps_y, reps_z) - 1, 2)),
+            pltpu.SemaphoreType.DMA((2, 2)),
+            pltpu.SemaphoreType.DMA((2, max(reps_y, reps_z) - 1, 2)),
+            pltpu.SemaphoreType.DMA((2, max(reps_y, reps_z) - 1, 2)),
         ],
         compiler_params=pltpu.CompilerParams(
             collective_id=0,
@@ -599,14 +655,21 @@
         momentum_up,
         momentum_down,
     )
+    results = pl.pallas_call(
+        functools.partial(hand_over, len(results)),
+        out_shape=tuple(jax.ShapeDtypeStruct(r.shape, r.dtype) for r in results),
+        in_specs=[vmem] * len(results),
+        out_specs=tuple([vmem] * len(results)),
+        name="hand_over",
+    )(*results)
     merged_up, merged_down, c_up, c_down, v_up, v_down, loss = results
     return merged_up[None], merged_down[None], c_up, c_down, v_up, v_down, loss[None]
 
 
 def solution(mesh):
     reps = mesh.shape["rep"]
-    reps_xy = 8 if reps % 8 == 0 and reps > 8 else 2
-    reps_z = reps // reps_xy
+    reps_y = 4 if reps % 16 == 0 else 2
+    reps_z = reps // (2 * reps_y)
     placed = (
         P("rep", None, "fsdp", None),
         P("rep", None, "fsdp", None),
@@ -625,7 +688,7 @@
         P(),
     )
     return jax.shard_map(
-        functools.partial(per_device, reps_z, reps_xy),
+        functools.partial(per_device, reps_z, reps_y),
         mesh=mesh,
         in_specs=placed,
         out_specs=(

time: 122 us -> 101 us (0.83)
  the two profiles are of different devices: /device:TPU:30 before, /device:TPU:50 now
where the time goes in v2:
time: 101 us; the launch traced here: 100 us
  Pallas kernels  99.1 us (98%)
  between operations  1.29 us (1%)
    pallas_call x1, Pallas kernels, per_device(): pl.pallas_call(functools.partial(kernel, reps_z, reps_y), out_shape=(jax....  96.8 us
    pallas_call x1, Pallas kernels, per_device(): pl.pallas_call(functools.partial(hand_over, len(results)), out_shape=tupl...  2.26 us

profile of v2, /device:TPU:50, one launch (start us, length us, event | category | flops | bytes accessed | tf_op | source)
XLA Modules:
  0.0 100.4 jit_solution(9368624983145194626)
XLA Ops:
  1.3 96.8 %window.1 = (bf16[2048,128]{1,0:T(8,128)(2,1)}, bf16[2048,128]{1,0:T(8,128)(2,1)}, f32[32,128]{1,0:T(8,128)}, f32[32,128]{1,0:T(8,128)}, f32[32,128]{1,0:T(8,128)}, /*index=5*/f32[32,128]{1,0:T(8,128)}, f32[2,128]{1,0:T(2,128)}) custom-call(s32[1]{0:T(128)S(6)} %copy.22.frag, bf16[2,128,2048]{2,1,0:T(8,128)(2,1)} %bitcast.11, ...), custom_call_target="tpu_custom_call" | custom-call | flops 13153337344 | bytes 10000000 | tf_op jit(solution)/shard_map/window/pallas_call | solution.py:578
  98.1 2.3 %hand_over.1 = (bf16[2048,128]{1,0:T(8,128)(2,1)}, bf16[2048,128]{1,0:T(8,128)(2,1)}, f32[32,128]{1,0:T(8,128)}, f32[32,128]{1,0:T(8,128)}, f32[32,128]{1,0:T(8,...) custom-call(bf16[2048,128]{1,0:T(8,128)(2,1)} %get-tuple-element.21.refs_0_, bf16[2048,128]{1,0:T(8,128)(2,1)} %get-tuple-element.22.refs_1_, ...), custom_call_target="tpu_custom_call" | custom-call | tf_op jit(solution)/shard_map/hand_over/pallas_call | solution.py:658

commit v3 on v2

--- a/solution.py
+++ b/solution.py
@@ -19,6 +19,8 @@
 F32 = jnp.float32
 BF16 = jnp.bfloat16
 CHUNKS = 4
+GROUPS = 2
+FEATS = (2, 2)
 
 
 def mm(a, b):
@@ -41,8 +43,8 @@
     reps_z,
     reps_y,
     frag,
-    x_in,
-    cot,
+    x_hbm,
+    cot_hbm,
     mid_gain,
     out_gain,
     up_hbm,
@@ -62,6 +64,8 @@
     velocity_up,
     velocity_down,
     loss,
+    x_in,
+    cot,
     up,
     down,
     x0,
@@ -88,6 +92,7 @@
     down_from_y,
     pair,
     from_x,
+    outer_in,
     central,
     rows_out,
     rows_in,
@@ -101,14 +106,17 @@
     c_sem,
     e_sem,
     f_sem,
+    o_sem,
 ):
     width, units_here = up.shape
-    tok = x_in.shape[1]
+    tok = x_hbm.shape[1]
     shards = 4
     units = units_here * shards
     tokens = tok * shards
     reps = reps_z * 2 * reps_y
-    half = 2 * tok
+    group = tokens // GROUPS
+    share = tok // GROUPS
+    per_group = CHUNKS // GROUPS
     bw = block.shape[4]
 
     rep = lax.axis_index("rep")
@@ -144,11 +152,6 @@
         sent.append(copy)
         return copy
 
-    load_up = pltpu.make_async_copy(up_hbm, up, load_sem.at[0])
-    load_down = pltpu.make_async_copy(down_hbm, down, load_sem.at[1])
-    load_up.start()
-    load_down.start()
-
     barrier = pltpu.get_barrier_semaphore()
     partners = [sib, peer, diag]
     partners += [device(o, xh, y) for o in others_z]
@@ -159,43 +162,60 @@
             barrier, inc=1, device_id=partner, device_id_type=pl.DeviceIdType.MESH
         )
 
+    loads = [
+        pltpu.make_async_copy(src, dst, load_sem.at[i])
+        for i, (src, dst) in enumerate(
+            (
+                (x_hbm.at[0], x_in.at[0]),
+                (up_hbm, up),
+                (down_hbm, down),
+                (x_hbm.at[1], x_in.at[1]),
+                (cot_hbm, cot),
+            )
+        )
+    ]
+    for load in loads:
+        load.start()
+
     rows_each = tok // CHUNKS
 
+    def at(c, slot):
+        return (c // per_group) * group + slot * share + (c % per_group) * rows_each
+
+    def piece(c, slot):
+        return pl.ds(at(c, slot), rows_each)
+
     def normalize_chunk(batch, dst, c):
-        rows = slice(c * rows_each, (c + 1) * rows_each)
-        v = x_in[batch, rows, :].astype(F32)
+        v = x_in[batch, c * rows_each : (c + 1) * rows_each, :].astype(F32)
         factor = lax.rsqrt(jnp.mean(v * v, axis=-1, keepdims=True) + norm_epsilon)
-        dst[rows, :] = (v * factor * mid_gain[...]).astype(BF16)
+        dst[piece(c, 0), :] = (v * factor * mid_gain[...]).astype(BF16)
 
     def spread(buf, g, c):
-        r = pl.ds(c * rows_each, rows_each)
         over = send(
-            buf.at[r, :],
-            buf.at[pl.ds(half + c * rows_each, rows_each), :],
-            gather_sem.at[g, 1, c],
-            peer,
+            buf.at[piece(c, 0), :], buf.at[piece(c, 2), :], gather_sem.at[g, 1, c], peer
         )
         near = send(
-            buf.at[r, :],
-            buf.at[pl.ds(tok + c * rows_each, rows_each), :],
-            gather_sem.at[g, 0, c],
-            sib,
+            buf.at[piece(c, 0), :], buf.at[piece(c, 1), :], gather_sem.at[g, 0, c], sib
         )
         return near, over
 
-    def forward(buf, g, c, over):
-        over.wait_recv()
+    def forward(buf, g, c, pairs):
+        pairs[c][1].wait_recv()
         return send(
-            buf.at[pl.ds(half + c * rows_each, rows_each), :],
-            buf.at[pl.ds(half + tok + c * rows_each, rows_each), :],
-            gather_sem.at[g, 2, c],
-            sib,
-        )
-
-    for c in range(CHUNKS):
+            buf.at[piece(c, 2), :], buf.at[piece(c, 3), :], gather_sem.at[g, 2, c], sib
+        )
+
+    def members(gr):
+        return range(gr * per_group, (gr + 1) * per_group)
+
+    loads[0].wait()
+    for c in range(per_group):
         normalize_chunk(0, x0, c)
     pl.semaphore_wait(barrier, len(partners))
-    pairs0 = [spread(x0, 0, c) for c in range(CHUNKS)]
+    pairs0 = [spread(x0, 0, c) for c in range(per_group)]
+    for c in range(per_group, CHUNKS):
+        normalize_chunk(0, x0, c)
+        pairs0.append(spread(x0, 0, c))
 
     chosen = [jnp.where(frag[0] == k, 1.0, 0.0) for k in range(units_here // bw)]
 
@@ -209,8 +229,8 @@
             picked = term if picked is None else picked + term
         return picked
 
-    load_up.wait()
-    load_down.wait()
+    for load in loads[1:]:
+        load.wait()
     span = width // reps
     slab = reps_y * span
     for k in range(0, width, slab):
@@ -271,28 +291,29 @@
         for i in range(reps_y - 1):
             total = total + down_from_y[i]
         pair[:, 1] = total
-        return send(pair.at[1 - xh], from_x, c_sem.at[0], across)
+        return send(pair, from_x, c_sem.at[0], across)
 
     def outer_step(copy):
-        copy.wait_recv()
+        for other in outer_copies + [copy]:
+            other.wait_recv()
         for w, (anchor, moment, cent_out, vel_out) in enumerate(
             (
                 (anchor_up, moment_up, central_up, velocity_up),
                 (anchor_down, moment_down, central_down, velocity_down),
             )
         ):
-            total = pair[xh, w] + from_x[w]
-            drift = anchor[...] - total / reps
-            velocity = outer_momentum * moment[...] + drift
-            cent = anchor[...] - outer_rate * (drift + outer_momentum * velocity)
-            vel_out[...] = velocity
-            cent_out[...] = cent
-            central[w, z * 2 + xh, y] = cent
-        mine = central.at[:, z * 2 + xh, y]
-        return send(mine, mine, c_sem.at[1], across)
-
-    def gather_once(copy):
-        copy.wait_recv()
+            for own in (True, False):
+                row = xh if own else 1 - xh
+                start = anchor[...] if own else outer_in[2 * w]
+                speed = moment[...] if own else outer_in[2 * w + 1]
+                total = pair[row, w] + from_x[row, w]
+                drift = start - total / reps
+                velocity = outer_momentum * speed + drift
+                cent = start - outer_rate * (drift + outer_momentum * velocity)
+                central[w, z * 2 + row, y] = cent
+                if own:
+                    vel_out[...] = velocity
+                    cent_out[...] = cent
         up_here = central.at[0, here, y]
         down_here = central.at[1, here, y]
         over_z = [
@@ -324,6 +345,10 @@
         return out
 
     block_copies = spread_blocks()
+    outer_copies = [
+        send(src, outer_in.at[i], o_sem.at[i], across)
+        for i, src in enumerate((anchor_up, moment_up, anchor_down, moment_down))
+    ]
 
     def hidden_of(buf, lo, count, keep_slope):
         rows = slice(lo, lo + count)
@@ -336,67 +361,43 @@
                     sig * (1 + pre * (1 - sig)) * (1.0 / math.sqrt(width))
                 )
 
-    feats = width // CHUNKS
-
-    def branch_of(lo, count, j):
+    def branch_of(lo, count, j, pieces_n):
+        feats = width // pieces_n
         part[lo : lo + count, j * feats : (j + 1) * feats] = mm_nt(
             hid[lo : lo + count, :], down[j * feats : (j + 1) * feats, :]
         )
 
-    def sib_send(b, which, j, dst):
-        lo = tok + which * half
+    def sib_send(b, which, gr, j, dst):
+        feats = width // FEATS[b]
         cols = pl.ds(j * feats, feats)
         return send(
-            part.at[pl.ds(lo, tok), cols],
-            dst.at[which, :, cols],
-            part_sem.at[b, which, j],
+            part.at[pl.ds(gr * group + (1 + 2 * which) * share, share), cols],
+            dst.at[which, pl.ds(gr * share, share), cols],
+            part_sem.at[b, which, gr * FEATS[b] + j],
             sib,
         )
 
-    def peer_send(b, j, copy, src_sib, staged, dst):
+    def peer_send(b, gr, j, copy, src_sib, staged, dst):
         copy.wait_recv()
+        feats = width // FEATS[b]
         cols = slice(j * feats, (j + 1) * feats)
-        staged[:, cols] = (part[half : half + tok, cols] + src_sib[1, :, cols]).astype(BF16)
-        ds = pl.ds(j * feats, feats)
-        return send(staged.at[:, ds], dst.at[:, ds], part_sem.at[b, 2, j], peer)
+        lo = gr * group + 2 * share
+        rows = slice(gr * share, (gr + 1) * share)
+        staged[rows, cols] = (
+            part[lo : lo + share, cols] + src_sib[1, rows, cols]
+        ).astype(BF16)
+        there = (pl.ds(gr * share, share), pl.ds(j * feats, feats))
+        return send(
+            staged.at[there], dst.at[there], part_sem.at[b, 2, gr * FEATS[b] + j], peer
+        )
 
     def lanes_of(column_vector):
         wide = jnp.broadcast_to(column_vector, (tok, 128))
         return jnp.transpose(wide)[0:1, :]
 
-    for near, _ in pairs0:
-        near.wait_recv()
-    hidden_of(x0, 0, half, True)
-    diag0 = []
-    near_part0 = []
-    for j in range(CHUNKS):
-        branch_of(0, half, j)
-        near_part0.append(sib_send(0, 0, j, from_sib0))
-        diag0.append(forward(x0, 0, j, pairs0[j][1]))
-    for copy in diag0:
-        copy.wait_recv()
-    hidden_of(x0, half, half, True)
-    far_part0 = []
-    over_part0 = []
-    for j in range(CHUNKS):
-        branch_of(half, half, j)
-        far_part0.append(sib_send(0, 1, j, from_sib0))
-        if j:
-            over_part0.append(
-                peer_send(0, j - 1, far_part0[j - 1], from_sib0, to_peer0, from_peer0)
-            )
-    over_part0.append(
-        peer_send(0, CHUNKS - 1, far_part0[-1], from_sib0, to_peer0, from_peer0)
-    )
-    for c in range(CHUNKS):
-        normalize_chunk(1, x1, c)
-    b_copies = sum_once(block_copies)
-    for copy in near_part0 + over_part0:
-        copy.wait_recv()
-
     def output_of(b, c, src_sib, src_peer):
         rows = slice(c * rows_each, (c + 1) * rows_each)
-        branch = part[rows, :] + src_sib[0, rows, :] + src_peer[rows, :].astype(F32)
+        branch = part[piece(c, 0), :] + src_sib[0, rows, :] + src_peer[rows, :].astype(F32)
         output = x_in[b, rows, :].astype(F32) + branch * (1.0 / math.sqrt(units))
         q = lax.rsqrt(jnp.mean(output * output, axis=-1, keepdims=True) + norm_epsilon)
         c_gain = cot[b, rows, :].astype(F32) * out_gain[...]
@@ -406,19 +407,57 @@
     def token_losses(columns):
         return lanes_of(jnp.concatenate(columns, axis=0))
 
+    near0 = [[] for _ in range(GROUPS)]
+    far0 = [[] for _ in range(GROUPS)]
+    over0 = [[] for _ in range(GROUPS)]
     pairs_d = []
     losses = []
+    diag0 = [forward(x0, 0, c, pairs0) for c in members(0)]
+
+    def layer_group(gr):
+        for c in members(gr):
+            pairs0[c][0].wait_recv()
+            diag0[c].wait_recv()
+        hidden_of(x0, gr * group, group, True)
+        n = FEATS[0]
+        for j in range(n):
+            branch_of(gr * group, group, j, n)
+            far0[gr].append(sib_send(0, 1, gr, j, from_sib0))
+            near0[gr].append(sib_send(0, 0, gr, j, from_sib0))
+            if j:
+                over0[gr].append(
+                    peer_send(
+                        0, gr, j - 1, far0[gr][j - 1], from_sib0, to_peer0, from_peer0
+                    )
+                )
+        if gr + 1 < GROUPS:
+            for c in members(gr + 1):
+                diag0.append(forward(x0, 0, c, pairs0))
+        over0[gr].append(
+            peer_send(0, gr, n - 1, far0[gr][n - 1], from_sib0, to_peer0, from_peer0)
+        )
+
+    def backward_group(gr):
+        for copy in near0[gr] + over0[gr]:
+            copy.wait_recv()
+        for c in members(gr):
+            output, q, c_gain, dotted = output_of(0, c, from_sib0, from_peer0)
+            losses.append(dotted * q)
+            g = c_gain * (1.0 / tokens)
+            doutput = q * g - output * (q * q * q * (dotted * (1.0 / (tokens * width))))
+            db[piece(c, 0), :] = (doutput * (1.0 / math.sqrt(units))).astype(BF16)
+            pairs_d.append(spread(db, 1, c))
+
+    layer_group(0)
     for c in range(CHUNKS):
-        output, q, c_gain, dotted = output_of(0, c, from_sib0, from_peer0)
-        losses.append(dotted * q)
-        g = c_gain * (1.0 / tokens)
-        doutput = q * g - output * (q * q * q * (dotted * (1.0 / (tokens * width))))
-        db[c * rows_each : (c + 1) * rows_each, :] = (
-            doutput * (1.0 / math.sqrt(units))
-        ).astype(BF16)
-        pairs_d.append(spread(db, 1, c))
+        normalize_chunk(1, x1, c)
+    layer_group(1)
+    b_copies = sum_once(block_copies)
+    backward_group(0)
+    pairs1 = [spread(x1, 2, 0)]
+    backward_group(1)
+    c_copy = sum_twice(b_copies)
     loss[0:1, :] = token_losses(losses)
-    c_copy = sum_twice(b_copies)
 
     def dpre_of(lo, count):
         rows = slice(lo, lo + count)
@@ -426,24 +465,30 @@
             dh = mm(db[rows, :], down[:, n : n + size])
             dpre[rows, n : n + size] = (dh * slope[rows, n : n + size]).astype(BF16)
 
-    step = 256
+    step = min(1024, width)
     n_steps = width // step
 
-    def first_half(dst, left, right):
+    def gradient(gr, dst, left, right):
+        lo = gr * group
+
         def body(i, carry):
             k = pl.multiple_of(i * step, step)
-            dst[pl.ds(k, step), :] = mm_tn(left[0:half, pl.ds(k, step)], right[0:half, :])
+            g = mm_tn(left[lo : lo + group, pl.ds(k, step)], right[lo : lo + group, :])
+            if gr:
+                g = g + dst[pl.ds(k, step), :]
+            dst[pl.ds(k, step), :] = g
             return carry
 
         lax.fori_loop(0, n_steps, body, 0)
 
-    def second_half(w, dst, left, right):
+    def last_gradient(w, dst, left, right):
+        lo = (GROUPS - 1) * group
         cols_acc[w] = jnp.zeros((1, units_here), F32)
 
         def body(i, carry):
             k = pl.multiple_of(i * step, step)
             g = dst[pl.ds(k, step), :] + mm_tn(
-                left[half : 2 * half, pl.ds(k, step)], right[half : 2 * half, :]
+                left[lo : lo + group, pl.ds(k, step)], right[lo : lo + group, :]
             )
             dst[pl.ds(k, step), :] = g
             sq = g * g
@@ -462,25 +507,26 @@
             for i, target in enumerate((sib, peer, diag))
         ]
 
-    for near, _ in pairs_d:
-        near.wait_recv()
-    dpre_of(0, half)
-    diag_d = [forward(db, 1, 0, pairs_d[0][1])]
-    first_half(grad_up, x0, dpre)
-    diag_d.append(forward(db, 1, 1, pairs_d[1][1]))
-    first_half(grad_down, db, hid)
-    for c in range(2, CHUNKS):
-        diag_d.append(forward(db, 1, c, pairs_d[c][1]))
-    d_copy = outer_step(c_copy)
-    for copy in diag_d:
-        copy.wait_recv()
-    pairs1 = [spread(x1, 2, c) for c in range(CHUNKS)]
-    dpre_of(half, half)
-    rows_up_copies = second_half(0, grad_up, x0, dpre)
-    e_copies = gather_once(d_copy)
-    diag1 = [forward(x1, 2, c, pairs1[c][1]) for c in range(2)]
-    rows_down_copies = second_half(1, grad_down, db, hid)
+    diag_d = [forward(db, 1, c, pairs_d) for c in members(0)]
+    for c in members(0):
+        pairs_d[c][0].wait_recv()
+        diag_d[c].wait_recv()
+    dpre_of(0, group)
+    e_copies = outer_step(c_copy)
+    gradient(0, grad_up, x0, dpre)
+    diag_d.append(forward(db, 1, per_group, pairs_d))
+    pairs1.append(spread(x1, 2, 1))
+    gradient(0, grad_down, db, hid)
+    diag_d += [forward(db, 1, c, pairs_d) for c in members(1)[1:]]
+    pairs1 += [spread(x1, 2, c) for c in range(2, CHUNKS)]
+    for c in members(1):
+        pairs_d[c][0].wait_recv()
+        diag_d[c].wait_recv()
+    dpre_of(group, group)
+    rows_up_copies = last_gradient(0, grad_up, x0, dpre)
     f_copies = gather_twice(e_copies)
+    diag1 = [forward(x1, 2, 0, pairs1)]
+    rows_down_copies = last_gradient(1, grad_down, db, hid)
 
     def factors(w, copies, rows_ref, cols_ref):
         for copy in copies:
@@ -503,40 +549,52 @@
                 old * (1 - inner_rate * weight_decay) - move
             ).astype(BF16)
 
-    def update_all(w, weight, grad):
+    def update_rows(w, weight, grad, lo, count):
+        strip = min(count, 256)
+
         def body(i, carry):
-            update(w, weight, grad, pl.multiple_of(i * step, step), step)
+            update(w, weight, grad, pl.multiple_of(lo + i * strip, strip), strip)
             return carry
 
-        lax.fori_loop(0, n_steps, body, 0)
+        lax.fori_loop(0, count // strip, body, 0)
 
     factors(0, rows_up_copies, up_rows, up_cols)
-    update_all(0, up, grad_up)
-    diag1 += [forward(x1, 2, c, pairs1[c][1]) for c in range(2, CHUNKS)]
-    for (near, _), far in zip(pairs1, diag1):
-        near.wait_recv()
-        far.wait_recv()
-    hidden_of(x1, 0, 2 * half, False)
-    factors(1, rows_down_copies, down_rows, down_cols)
-    for copy in near_part0 + far_part0:
-        copy.wait_send()
-        sent[:] = [other for other in sent if other is not copy]
-    near_part1 = []
-    far_part1 = []
-    over_part1 = []
-    for j in range(CHUNKS):
-        for k, size in pieces(feats, step):
-            update(1, down, grad_down, j * feats + k, size)
-        branch_of(0, 2 * half, j)
-        far_part1.append(sib_send(1, 1, j, from_sib1))
-        near_part1.append(sib_send(1, 0, j, from_sib1))
-        if j:
-            over_part1.append(
-                peer_send(1, j - 1, far_part1[j - 1], from_sib1, to_peer1, from_peer1)
-            )
-    over_part1.append(
-        peer_send(1, CHUNKS - 1, far_part1[-1], from_sib1, to_peer1, from_peer1)
-    )
+    update_rows(0, up, grad_up, 0, width)
+    diag1 += [forward(x1, 2, c, pairs1) for c in members(0)[1:]]
+    for gr in range(GROUPS):
+        for copy in near0[gr] + far0[gr]:
+            copy.wait_send()
+            sent[:] = [other for other in sent if other is not copy]
+
+    near1 = []
+    over1 = []
+
+    def second_group(gr):
+        for c in members(gr):
+            pairs1[c][0].wait_recv()
+            diag1[c].wait_recv()
+        hidden_of(x1, gr * group, group, False)
+        n = FEATS[1]
+        far = []
+        if gr == 0:
+            factors(1, rows_down_copies, down_rows, down_cols)
+        for j in range(n):
+            if gr == 0:
+                update_rows(1, down, grad_down, j * (width // n), width // n)
+            branch_of(gr * group, group, j, n)
+            far.append(sib_send(1, 1, gr, j, from_sib1))
+            near1.append(sib_send(1, 0, gr, j, from_sib1))
+            if j:
+                over1.append(
+                    peer_send(1, gr, j - 1, far[j - 1], from_sib1, to_peer1, from_peer1)
+                )
+        if gr + 1 < GROUPS:
+            for c in members(gr + 1):
+                diag1.append(forward(x1, 2, c, pairs1))
+        over1.append(peer_send(1, gr, n - 1, far[n - 1], from_sib1, to_peer1, from_peer1))
+
+    for gr in range(GROUPS):
+        second_group(gr)
 
     for copy in f_copies:
         copy.wait_recv()
@@ -547,7 +605,7 @@
                 + (1 - mixing) * central[w, k // slab].reshape(slab, bw)
             ).astype(BF16)
 
-    for copy in near_part1 + over_part1:
+    for copy in near1 + over1:
         copy.wait_recv()
     losses = []
     for c in range(CHUNKS):
@@ -586,9 +644,11 @@
             jax.ShapeDtypeStruct((span, bw), F32),
             jax.ShapeDtypeStruct((2, tok), F32),
         ),
-        in_specs=[smem, vmem, vmem, vmem, vmem, hbm, hbm] + [vmem] * 8,
+        in_specs=[smem, hbm, hbm, vmem, vmem, hbm, hbm] + [vmem] * 8,
         out_specs=tuple([vmem] * 7),
         scratch_shapes=[
+            pltpu.VMEM((2, tok, width), BF16),
+            pltpu.VMEM((2, tok, width), BF16),
             pltpu.VMEM((width, units_here), BF16),
             pltpu.VMEM((width, units_here), BF16),
             pltpu.VMEM((tokens, width), BF16),
@@ -614,20 +674,22 @@
             pltpu.VMEM((2, reps_y, span, bw), F32),
             pltpu.VMEM((reps_y - 1, 2, span, bw), F32),
             pltpu.VMEM((2, 2, span, bw), F32),
-            pltpu.VMEM((2, span, bw), F32),
+            pltpu.VMEM((2, 2, span, bw), F32),
+            pltpu.VMEM((4, span, bw), F32),
             pltpu.VMEM((2, 2 * reps_z, reps_y, span, bw), F32),
             pltpu.VMEM((2, 1, width), F32),
             pltpu.VMEM((2, 3, 1, width), F32),
             pltpu.VMEM((2, 1, units_here), F32),
-            pltpu.SemaphoreType.DMA((2,)),
+            pltpu.SemaphoreType.DMA((5,)),
             pltpu.SemaphoreType.DMA((3, 3, CHUNKS, 2)),
-            pltpu.SemaphoreType.DMA((2, 3, CHUNKS, 2)),
+            pltpu.SemaphoreType.DMA((2, 3, GROUPS * max(FEATS), 2)),
             pltpu.SemaphoreType.DMA((2, 3, 2)),
             pltpu.SemaphoreType.DMA((2, max(reps_y, reps_z) - 1, 2)),
             pltpu.SemaphoreType.DMA((2, max(reps_y, reps_z) - 1, 2)),
             pltpu.SemaphoreType.DMA((2, 2)),
             pltpu.SemaphoreType.DMA((2, max(reps_y, reps_z) - 1, 2)),
             pltpu.SemaphoreType.DMA((2, max(reps_y, reps_z) - 1, 2)),
+            pltpu.SemaphoreType.DMA((4, 2)),
         ],
         compiler_params=pltpu.CompilerParams(
             collective_id=0,

time: 101 us -> 93.5 us (0.926)
  the two profiles are of different devices: /device:TPU:50 before, /device:TPU:1 now
where the time goes in v3:
time: 93.5 us; the launch traced here: 93.4 us
  Pallas kernels  92.1 us (99%)
  between operations  1.29 us (1%)
    pallas_call x1, Pallas kernels, per_device(): pl.pallas_call(functools.partial(kernel, reps_z, reps_y), out_shape=(jax....  89.8 us
    pallas_call x1, Pallas kernels, per_device(): pl.pallas_call(functools.partial(hand_over, len(results)), out_shape=tupl...  2.26 us

profile of v3, /device:TPU:1, one launch (start us, length us, event | category | flops | bytes accessed | tf_op | source)
XLA Modules:
  0.0 93.4 jit_solution(5782345453462601189)
XLA Ops:
  1.3 89.8 %window.1 = (bf16[2048,128]{1,0:T(8,128)(2,1)}, bf16[2048,128]{1,0:T(8,128)(2,1)}, f32[32,128]{1,0:T(8,128)}, f32[32,128]{1,0:T(8,128)}, f32[32,128]{1,0:T(8,128)}, /*index=5*/f32[32,128]{1,0:T(8,128)}, f32[2,128]{1,0:T(2,128)}) custom-call(s32[1]{0:T(128)S(6)} %copy.22.frag, bf16[2,128,2048]{2,1,0:T(8,128)(2,1)} %bitcast.11, ...), custom_call_target="tpu_custom_call" | custom-call | flops 13153337344 | bytes 10000000 | tf_op jit(solution)/shard_map/window/pallas_call | solution.py:636
  91.1 2.3 %hand_over.1 = (bf16[2048,128]{1,0:T(8,128)(2,1)}, bf16[2048,128]{1,0:T(8,128)(2,1)}, f32[32,128]{1,0:T(8,128)}, f32[32,128]{1,0:T(8,128)}, f32[32,128]{1,0:T(8,...) custom-call(bf16[2048,128]{1,0:T(8,128)(2,1)} %get-tuple-element.21.refs_0_, bf16[2048,128]{1,0:T(8,128)(2,1)} %get-tuple-element.22.refs_1_, ...), custom_call_target="tpu_custom_call" | custom-call | tf_op jit(solution)/shard_map/hand_over/pallas_call | solution.py:720

commit v4 on v3

--- a/solution.py
+++ b/solution.py
@@ -18,7 +18,7 @@
 
 F32 = jnp.float32
 BF16 = jnp.bfloat16
-CHUNKS = 4
+CHUNKS = 2
 GROUPS = 2
 FEATS = (2, 2)
 
@@ -430,12 +430,12 @@
                         0, gr, j - 1, far0[gr][j - 1], from_sib0, to_peer0, from_peer0
                     )
                 )
+        over0[gr].append(
+            peer_send(0, gr, n - 1, far0[gr][n - 1], from_sib0, to_peer0, from_peer0)
+        )
         if gr + 1 < GROUPS:
             for c in members(gr + 1):
                 diag0.append(forward(x0, 0, c, pairs0))
-        over0[gr].append(
-            peer_send(0, gr, n - 1, far0[gr][n - 1], from_sib0, to_peer0, from_peer0)
-        )
 
     def backward_group(gr):
         for copy in near0[gr] + over0[gr]:
@@ -454,7 +454,7 @@
     layer_group(1)
     b_copies = sum_once(block_copies)
     backward_group(0)
-    pairs1 = [spread(x1, 2, 0)]
+    pairs1 = []
     backward_group(1)
     c_copy = sum_twice(b_copies)
     loss[0:1, :] = token_losses(losses)
@@ -515,7 +515,7 @@
     e_copies = outer_step(c_copy)
     gradient(0, grad_up, x0, dpre)
     diag_d.append(forward(db, 1, per_group, pairs_d))
-    pairs1.append(spread(x1, 2, 1))
+    pairs1 += [spread(x1, 2, c) for c in range(2)]
     gradient(0, grad_down, db, hid)
     diag_d += [forward(db, 1, c, pairs_d) for c in members(1)[1:]]
     pairs1 += [spread(x1, 2, c) for c in range(2, CHUNKS)]
@@ -588,10 +588,10 @@
                 over1.append(
                     peer_send(1, gr, j - 1, far[j - 1], from_sib1, to_peer1, from_peer1)
                 )
+        over1.append(peer_send(1, gr, n - 1, far[n - 1], from_sib1, to_peer1, from_peer1))
         if gr + 1 < GROUPS:
             for c in members(gr + 1):
                 diag1.append(forward(x1, 2, c, pairs1))
-        over1.append(peer_send(1, gr, n - 1, far[n - 1], from_sib1, to_peer1, from_peer1))
 
     for gr in range(GROUPS):
         second_group(gr)

time: 93.5 us -> 91.9 us (0.983)
  Pallas kernels: 92.1 us -> 90.4 us
    pallas_call x1, Pallas kernels: 89.8 us -> 88.1 us  [per_device(): pl.pallas_call(functools.partial(kernel, reps_z, reps_y), out_shape=(jax....]
where the time goes in v4:
time: 91.9 us; the launch traced here: 91.7 us
  Pallas kernels  90.4 us (98%)
  between operations  1.29 us (1%)
    pallas_call x1, Pallas kernels, per_device(): pl.pallas_call(functools.partial(kernel, reps_z, reps_y), out_shape=(jax....  88.1 us
    pallas_call x1, Pallas kernels, per_device(): pl.pallas_call(functools.partial(hand_over, len(results)), out_shape=tupl...  2.26 us

profile of v4, /device:TPU:1, one launch (start us, length us, event | category | flops | bytes accessed | tf_op | source)
XLA Modules:
  0.0 91.7 jit_solution(10635387355836633014)
XLA Ops:
  1.3 88.1 %window.1 = (bf16[2048,128]{1,0:T(8,128)(2,1)}, bf16[2048,128]{1,0:T(8,128)(2,1)}, f32[32,128]{1,0:T(8,128)}, f32[32,128]{1,0:T(8,128)}, f32[32,128]{1,0:T(8,128)}, /*index=5*/f32[32,128]{1,0:T(8,128)}, f32[2,128]{1,0:T(2,128)}) custom-call(s32[1]{0:T(128)S(6)} %copy.22.frag, bf16[2,128,2048]{2,1,0:T(8,128)(2,1)} %bitcast.11, ...), custom_call_target="tpu_custom_call" | custom-call | flops 13153337344 | bytes 10000000 | tf_op jit(solution)/shard_map/window/pallas_call | solution.py:636
  89.4 2.3 %hand_over.1 = (bf16[2048,128]{1,0:T(8,128)(2,1)}, bf16[2048,128]{1,0:T(8,128)(2,1)}, f32[32,128]{1,0:T(8,128)}, f32[32,128]{1,0:T(8,128)}, f32[32,128]{1,0:T(8,...) custom-call(bf16[2048,128]{1,0:T(8,128)(2,1)} %get-tuple-element.21.refs_0_, bf16[2048,128]{1,0:T(8,128)(2,1)} %get-tuple-element.22.refs_1_, ...), custom_call_target="tpu_custom_call" | custom-call | tf_op jit(solution)/shard_map/hand_over/pallas_call | solution.py:720

commit v5 on v4

--- a/solution.py
+++ b/solution.py
@@ -550,7 +550,7 @@
             ).astype(BF16)
 
     def update_rows(w, weight, grad, lo, count):
-        strip = min(count, 256)
+        strip = min(count, 512)
 
         def body(i, carry):
             update(w, weight, grad, pl.multiple_of(lo + i * strip, strip), strip)

time: 91.9 us -> 91.4 us (level)
  no operation moved by 1% of the time
where the time goes in v5:
time: 91.4 us; the launch traced here: 91.2 us
  Pallas kernels  89.9 us (98%)
  between operations  1.29 us (1%)
    pallas_call x1, Pallas kernels, per_device(): pl.pallas_call(functools.partial(kernel, reps_z, reps_y), out_shape=(jax....  87.7 us
    pallas_call x1, Pallas kernels, per_device(): pl.pallas_call(functools.partial(hand_over, len(results)), out_shape=tupl...  2.26 us

profile of v5, /device:TPU:1, one launch (start us, length us, event | category | flops | bytes accessed | tf_op | source)
XLA Modules:
  0.0 91.2 jit_solution(9259600529546351247)
XLA Ops:
  1.3 87.7 %window.1 = (bf16[2048,128]{1,0:T(8,128)(2,1)}, bf16[2048,128]{1,0:T(8,128)(2,1)}, f32[32,128]{1,0:T(8,128)}, f32[32,128]{1,0:T(8,128)}, f32[32,128]{1,0:T(8,128)}, /*index=5*/f32[32,128]{1,0:T(8,128)}, f32[2,128]{1,0:T(2,128)}) custom-call(s32[1]{0:T(128)S(6)} %copy.22.frag, bf16[2,128,2048]{2,1,0:T(8,128)(2,1)} %bitcast.11, ...), custom_call_target="tpu_custom_call" | custom-call | flops 13153337344 | bytes 10000000 | tf_op jit(solution)/shard_map/window/pallas_call | solution.py:636
  89.0 2.3 %hand_over.1 = (bf16[2048,128]{1,0:T(8,128)(2,1)}, bf16[2048,128]{1,0:T(8,128)(2,1)}, f32[32,128]{1,0:T(8,128)}, f32[32,128]{1,0:T(8,128)}, f32[32,128]{1,0:T(8,...) custom-call(bf16[2048,128]{1,0:T(8,128)(2,1)} %get-tuple-element.21.refs_0_, bf16[2048,128]{1,0:T(8,128)(2,1)} %get-tuple-element.22.refs_1_, ...), custom_call_target="tpu_custom_call" | custom-call | tf_op jit(solution)/shard_map/hand_over/pallas_call | solution.py:720
